TPU v7x, 32 devices: a whole 2x2x4 slice. The times are simulated.
32 devices in a mesh: freq: 4 (over z), rcv: 8 (over y, x, core).
Axes of the slice: x: 2, y: 2, z: 4, core: 2. Of those that a mesh axis runs over, the one named last changes fastest.
Arguments:
- reflection: bfloat16 [2, 96, 2048, 2048], P(None, 'freq', 'rcv'), may hold values from -0.4375 to 0.4375
- direct: float32 [24, 2048, 512], P('freq', 'rcv'), may hold values from -6 to 6
- onset_index: int32 [24, 2048], P('freq', 'rcv'), may hold values from 128 to 511
Outputs:
- focusing_plus: float32 [24, 2048, 512], P('freq', 'rcv')
- focusing_minus: float32 [24, 2048, 512], P('freq', 'rcv')
All inputs are finite; a program needn't handle non-finite values.
Results may differ from a plain program's by a relative error of at most 0.024.
Values may be sent and summed in bfloat16 or wider, within the bound.
A program may use at most 192 MiB of HBM per device.

v0:
```python
import math

import jax
import jax.numpy as jnp
from jax import lax
from jax.sharding import PartitionSpec as P

NF = 96
NT = 512
FLO = 8
ITERS = 3


def tables():
    samples = jnp.arange(NT, dtype=jnp.int32)
    bins = FLO + jnp.arange(NF, dtype=jnp.int32)
    phase = bins[:, None] * samples[None, :] % NT
    angles = phase.astype(jnp.float32) * (2.0 * math.pi / NT)
    return (jnp.cos(angles), jnp.sin(angles))


def to_spectrum(field, cosine, sine_table):
    highest = lax.Precision.HIGHEST
    real_part = jnp.einsum("ft,pst->fps", cosine, field, precision=highest)
    imag_part = -jnp.einsum("ft,pst->fps", sine_table, field, precision=highest)
    return jnp.stack([real_part, imag_part]).astype(jnp.bfloat16)


def to_time(fourier_spectrum, cosine, sine_table):
    highest = lax.Precision.HIGHEST
    values = fourier_spectrum.astype(jnp.float32)
    first = jnp.einsum("ft,fps->pst", cosine, values[0], precision=highest)
    second = jnp.einsum("ft,fps->pst", sine_table, values[1], precision=highest)
    return 2.0 / NT * (first - second)


def forward_block(refl_cols, spectra):
    reflectivity_real, reflectivity_imaginary = (refl_cols[0], refl_cols[1])
    spectral_real, spectral_imaginary = (spectra[0], spectra[1])
    real_part = jnp.einsum(
        "wna,wja->wjn", reflectivity_real, spectral_real, preferred_element_type=jnp.float32
    ) - jnp.einsum(
        "wna,wja->wjn",
        reflectivity_imaginary,
        spectral_imaginary,
        preferred_element_type=jnp.float32,
    )
    imag_part = jnp.einsum(
        "wna,wja->wjn", reflectivity_real, spectral_imaginary, preferred_element_type=jnp.float32
    ) + jnp.einsum(
        "wna,wja->wjn", reflectivity_imaginary, spectral_real, preferred_element_type=jnp.float32
    )
    return jnp.stack([real_part, imag_part])


def adjoint_block(reflection, spectra):
    reflectivity_real, reflectivity_imaginary = (reflection[0], reflection[1])
    spectral_real, spectral_imaginary = (spectra[0], spectra[1])
    real_part = jnp.einsum(
        "gmk,gim->gik", reflectivity_real, spectral_real, preferred_element_type=jnp.float32
    ) + jnp.einsum(
        "gmk,gim->gik",
        reflectivity_imaginary,
        spectral_imaginary,
        preferred_element_type=jnp.float32,
    )
    imag_part = jnp.einsum(
        "gmk,gim->gik", reflectivity_real, spectral_imaginary, preferred_element_type=jnp.float32
    ) - jnp.einsum(
        "gmk,gim->gik", reflectivity_imaginary, spectral_real, preferred_element_type=jnp.float32
    )
    return jnp.stack([real_part, imag_part])


def forward_image(reflection, fourier_spectrum):
    collected_rows = lax.all_gather(fourier_spectrum, "rcv", axis=3, tiled=True)
    band_limited = lax.all_to_all(collected_rows, "freq", split_axis=1, concat_axis=2, tiled=True)
    image = forward_block(reflection, band_limited)
    return lax.all_to_all(
        image.astype(jnp.bfloat16), "freq", split_axis=2, concat_axis=1, tiled=True
    )


def adjoint_image(reflection, fourier_spectrum):
    band_limited = lax.all_to_all(fourier_spectrum, "freq", split_axis=1, concat_axis=2, tiled=True)
    partial_sums = adjoint_block(reflection, band_limited)
    reduced_total = lax.psum_scatter(
        partial_sums.astype(jnp.bfloat16), "rcv", scatter_dimension=3, tiled=True
    )
    return lax.all_to_all(reduced_total, "freq", split_axis=2, concat_axis=1, tiled=True)


def local(reflection, direct, onset_index):
    cosine, sine_table = tables()
    samples = jnp.arange(NT, dtype=jnp.int32)
    window = (samples[None, None, :] < onset_index[:, :, None]).astype(jnp.float32)
    plus_field = direct
    minus_field = jnp.zeros_like(direct)
    for _ in range(ITERS):
        image = forward_image(reflection, to_spectrum(plus_field, cosine, sine_table))
        minus_field = window * to_time(image, cosine, sine_table)
        back_image = adjoint_image(reflection, to_spectrum(minus_field, cosine, sine_table))
        plus_field = direct + window * to_time(back_image, cosine, sine_table)
    return (plus_field, minus_field)


def solution(mesh):
    placed = (P(None, "freq", "rcv", None), P("freq", "rcv", None), P("freq", "rcv"))
    return jax.shard_map(
        local,
        mesh=mesh,
        in_specs=placed,
        out_specs=(P("freq", "rcv", None), P("freq", "rcv", None)),
        check_vma=False,
    )
```

profile of v0, /device:TPU:0, one launch (start us, length us, event | category | flops | bytes accessed | tf_op | source)
XLA Modules:
  0.0 1245.4 jit_solution(7349416584964236823)
XLA Ops:
  7.2 5.9 fusion.197
  18.0 42.5 %all-gather.4.cloned.1.call-done = bf16[2,96,6,2048]{3,1,2,0:T(8,128)(2,1)} async-done(((bf16[2,96,6,256]{3,1,2,0:T(8,128)(2,1)}), bf16[2,96,6,2048]{3,1,2,0:T(8,128)(2,1)}) %all-gather.4.cloned.1.call-update) | async-done | bytes 4718608 | tf_op jit(solution)/shard_map/all_gather | solution.py:76
  60.5 9.5 copy.203
  70.0 109.4 %all_to_all.180 = bf16[2,96,6,2048]{3,0,2,1:T(2,128)(2,1)S(1)} all-to-all(bf16[2,96,6,2048]{3,0,2,1:T(2,128)(2,1)} %copy.203), channel_id=1, replica_groups=mesh['freq'=4,'rcv'=8] {'freq'}, dimensions={1} | all-to-all | bytes 9437184 | tf_op jit(solution)/shard_map/all_to_all | solution.py:77
  185.5 13.2 %fusion.22 = f32[24,24,256]{2,1,0:T(8,128)} fusion(bf16[24,24,2048]{2,0,1:T(8,128)(2,1)} %bitcast.307, bf16[2,24,256,2048]{3,2,1,0:T(8,128)(2,1)} %param.3), kind=kOutput, calls=%fused_computation.22 | convolution fusion | flops 603979776 | bytes 28114944 | tf_op jit(solution)/shard_map/wna,wja->wjn/dot_general | solution.py:42
  198.7 13.2 %fusion.20 = f32[24,24,256]{2,1,0:T(8,128)} fusion(bf16[24,24,2048]{2,0,1:T(8,128)(2,1)} %bitcast.313, bf16[2,24,256,2048]{3,2,1,0:T(8,128)(2,1)} %param.3), kind=kOutput, calls=%fused_computation.20 | convolution fusion | flops 603979776 | bytes 28114944 | tf_op jit(solution)/shard_map/wna,wja->wjn/dot_general | solution.py:50
  211.8 12.6 %fusion.181 = bf16[1,24,24,256]{3,2,1,0:T(8,128)(2,1)S(1)} fusion(f32[24,24,256]{2,1,0:T(8,128)} %fusion.22, bf16[24,24,2048]{2,0,1:T(8,128)(2,1)} %bitcast.314, bf16[2,24,256,2048]{3,2,1,0:T(8,128)(2,1)} %param.3), kind=kOutput, calls=%fused_computation.117 | convolution fusion | flops 604274688 | bytes 28409856 | tf_op jit(solution)/shard_map/wna,wja->wjn/dot_general | solution.py:40
  224.4 13.3 %fusion.176 = bf16[1,24,24,256]{3,2,1,0:T(8,128)(2,1)} fusion(f32[24,24,256]{2,1,0:T(8,128)} %fusion.20, bf16[24,24,2048]{2,0,1:T(8,128)(2,1)} %bitcast.308, bf16[2,24,256,2048]{3,2,1,0:T(8,128)(2,1)} %param.3), kind=kOutput, calls=%fused_computation.116 | convolution fusion | flops 604274688 | bytes 28409856 | tf_op jit(solution)/shard_map/wna,wja->wjn/dot_general | solution.py:48
  238.9 18.2 %all_to_all.181 = bf16[2,24,24,256]{3,1,0,2:T(8,128)(2,1)S(1)} all-to-all(bf16[2,24,24,256]{3,1,0,2:T(8,128)(2,1)S(1)} %copy.211), channel_id=1, replica_groups=mesh['freq'=4,'rcv'=8] {'freq'}, dimensions={2} | all-to-all | bytes 1179648 | tf_op jit(solution)/shard_map/all_to_all | solution.py:79
  270.5 17.7 %all_to_all.182 = bf16[2,96,6,256]{3,0,2,1:T(2,128)(2,1)S(1)} all-to-all(bf16[2,96,6,256]{3,0,2,1:T(2,128)(2,1)S(1)} %copy.215), channel_id=1, replica_groups=mesh['freq'=4,'rcv'=8] {'freq'}, dimensions={1} | all-to-all | bytes 1179648 | tf_op jit(solution)/shard_map/all_to_all | solution.py:85
  288.5 12.3 fusion.16
  300.8 9.9 fusion.18
  310.7 12.7 %fusion.63 = bf16[1,24,24,2048]{3,2,1,0:T(8,128)(2,1)} fusion(f32[24,24,2048]{2,1,0:T(8,128)} %fusion.16, bf16[24,24,256]{2,0,1:T(8,128)(2,1)S(1)} %bitcast.296, bf16[2,24,256,2048]{3,2,1,0:T(8,128)(2,1)} %param.3), kind=kOutput, calls=%fused_computation.65 | convolution fusion | flops 606339072 | bytes 32538624 | tf_op jit(solution)/shard_map/gmk,gim->gik/dot_general | solution.py:67
  323.4 11.5 fusion.60
  335.0 4.9 pad_maximum_fusion
  340.0 52.1 %reduce-scatter.4.cloned.1.call-done = bf16[2,24,24,256]{3,2,1,0:T(8,128)(2,1)} async-done(((bf16[2,24,24,2048]{3,2,1,0:T(8,128)(2,1)}), bf16[2,24,24,256]{3,2,1,0:T(8,128)(2,1)}) %reduce-scatter.4.cloned.1.call-update) | async-done | bytes 589840 | tf_op jit(solution)/shard_map/reduce_scatter | solution.py:87
  393.3 20.7 %all_to_all.183 = bf16[2,24,24,256]{3,1,0,2:T(8,128)(2,1)S(1)} all-to-all(bf16[2,24,24,256]{3,1,0,2:T(8,128)(2,1)S(1)} %copy.223), channel_id=1, replica_groups=mesh['freq'=4,'rcv'=8] {'freq'}, dimensions={2} | all-to-all | bytes 1179648 | tf_op jit(solution)/shard_map/all_to_all | solution.py:90
  428.1 37.8 %all-gather.6.cloned.1.call-done = bf16[2,96,6,2048]{3,1,2,0:T(8,128)(2,1)} async-done(((bf16[2,96,6,256]{3,1,2,0:T(8,128)(2,1)}), bf16[2,96,6,2048]{3,1,2,0:T(8,128)(2,1)}) %all-gather.6.cloned.1.call-update) | async-done | bytes 4718608 | tf_op jit(solution)/shard_map/all_gather | solution.py:76
  465.8 9.5 copy.227
  475.3 109.4 %all_to_all.184 = bf16[2,96,6,2048]{3,0,2,1:T(2,128)(2,1)S(1)} all-to-all(bf16[2,96,6,2048]{3,0,2,1:T(2,128)(2,1)} %copy.227), channel_id=1, replica_groups=mesh['freq'=4,'rcv'=8] {'freq'}, dimensions={1} | all-to-all | bytes 9437184 | tf_op jit(solution)/shard_map/all_to_all | solution.py:77
  590.7 13.2 %fusion.14 = f32[24,24,256]{2,1,0:T(8,128)} fusion(bf16[24,24,2048]{2,0,1:T(8,128)(2,1)} %bitcast.309, bf16[2,24,256,2048]{3,2,1,0:T(8,128)(2,1)} %param.3), kind=kOutput, calls=%fused_computation.14 | convolution fusion | flops 603979776 | bytes 28114944 | tf_op jit(solution)/shard_map/wna,wja->wjn/dot_general | solution.py:42
  607.2 13.2 %fusion.12 = f32[24,24,256]{2,1,0:T(8,128)} fusion(bf16[24,24,2048]{2,0,1:T(8,128)(2,1)} %bitcast.315, bf16[2,24,256,2048]{3,2,1,0:T(8,128)(2,1)} %param.3), kind=kOutput, calls=%fused_computation.12 | convolution fusion | flops 603979776 | bytes 28114944 | tf_op jit(solution)/shard_map/wna,wja->wjn/dot_general | solution.py:50
  620.3 12.8 %fusion.171 = bf16[1,24,24,256]{3,2,1,0:T(8,128)(2,1)S(1)} fusion(f32[24,24,256]{2,1,0:T(8,128)} %fusion.14, bf16[24,24,2048]{2,0,1:T(8,128)(2,1)} %bitcast.316, bf16[2,24,256,2048]{3,2,1,0:T(8,128)(2,1)} %param.3), kind=kOutput, calls=%fused_computation.115 | convolution fusion | flops 604274688 | bytes 28409856 | tf_op jit(solution)/shard_map/wna,wja->wjn/dot_general | solution.py:40
  633.1 13.3 %fusion.166 = bf16[1,24,24,256]{3,2,1,0:T(8,128)(2,1)} fusion(f32[24,24,256]{2,1,0:T(8,128)} %fusion.12, bf16[24,24,2048]{2,0,1:T(8,128)(2,1)} %bitcast.310, bf16[2,24,256,2048]{3,2,1,0:T(8,128)(2,1)} %param.3), kind=kOutput, calls=%fused_computation.114 | convolution fusion | flops 604274688 | bytes 28409856 | tf_op jit(solution)/shard_map/wna,wja->wjn/dot_general | solution.py:48
  647.6 18.4 %all_to_all.185 = bf16[2,24,24,256]{3,1,0,2:T(8,128)(2,1)S(1)} all-to-all(bf16[2,24,24,256]{3,1,0,2:T(8,128)(2,1)S(1)} %copy.235), channel_id=1, replica_groups=mesh['freq'=4,'rcv'=8] {'freq'}, dimensions={2} | all-to-all | bytes 1179648 | tf_op jit(solution)/shard_map/all_to_all | solution.py:79
  679.4 17.7 %all_to_all.186 = bf16[2,96,6,256]{3,0,2,1:T(2,128)(2,1)S(1)} all-to-all(bf16[2,96,6,256]{3,0,2,1:T(2,128)(2,1)S(1)} %copy.239), channel_id=1, replica_groups=mesh['freq'=4,'rcv'=8] {'freq'}, dimensions={1} | all-to-all | bytes 1179648 | tf_op jit(solution)/shard_map/all_to_all | solution.py:85
  697.4 12.3 fusion.8
  709.7 9.9 fusion.10
  719.6 12.7 %fusion.69 = bf16[1,24,24,2048]{3,2,1,0:T(8,128)(2,1)} fusion(f32[24,24,2048]{2,1,0:T(8,128)} %fusion.8, bf16[24,24,256]{2,0,1:T(8,128)(2,1)S(1)} %bitcast.300, bf16[2,24,256,2048]{3,2,1,0:T(8,128)(2,1)} %param.3), kind=kOutput, calls=%fused_computation.67 | convolution fusion | flops 606339072 | bytes 32538624 | tf_op jit(solution)/shard_map/gmk,gim->gik/dot_general | solution.py:67
  732.3 11.5 fusion.66
  743.8 4.9 pad_maximum_fusion.1
  748.9 52.2 %reduce-scatter.6.cloned.1.call-done = bf16[2,24,24,256]{3,2,1,0:T(8,128)(2,1)} async-done(((bf16[2,24,24,2048]{3,2,1,0:T(8,128)(2,1)}), bf16[2,24,24,256]{3,2,1,0:T(8,128)(2,1)}) %reduce-scatter.6.cloned.1.call-update) | async-done | bytes 589840 | tf_op jit(solution)/shard_map/reduce_scatter | solution.py:87
  802.2 20.5 %all_to_all.187 = bf16[2,24,24,256]{3,1,0,2:T(8,128)(2,1)S(1)} all-to-all(bf16[2,24,24,256]{3,1,0,2:T(8,128)(2,1)S(1)} %copy.247), channel_id=1, replica_groups=mesh['freq'=4,'rcv'=8] {'freq'}, dimensions={2} | all-to-all | bytes 1179648 | tf_op jit(solution)/shard_map/all_to_all | solution.py:90
  837.0 37.6 %all-gather.8.cloned.1.call-done = bf16[2,96,6,2048]{3,1,2,0:T(8,128)(2,1)} async-done(((bf16[2,96,6,256]{3,1,2,0:T(8,128)(2,1)}), bf16[2,96,6,2048]{3,1,2,0:T(8,128)(2,1)}) %all-gather.8.cloned.1.call-update) | async-done | bytes 4718608 | tf_op jit(solution)/shard_map/all_gather | solution.py:76
  874.5 9.5 copy.251
  884.0 109.4 %all_to_all.188 = bf16[2,96,6,2048]{3,0,2,1:T(2,128)(2,1)S(1)} all-to-all(bf16[2,96,6,2048]{3,0,2,1:T(2,128)(2,1)} %copy.251), channel_id=1, replica_groups=mesh['freq'=4,'rcv'=8] {'freq'}, dimensions={1} | all-to-all | bytes 9437184 | tf_op jit(solution)/shard_map/all_to_all | solution.py:77
  999.3 13.2 %fusion.6 = f32[24,24,256]{2,1,0:T(8,128)} fusion(bf16[24,24,2048]{2,0,1:T(8,128)(2,1)} %bitcast.311, bf16[2,24,256,2048]{3,2,1,0:T(8,128)(2,1)} %param.3), kind=kOutput, calls=%fused_computation.6 | convolution fusion | flops 603979776 | bytes 28114944 | tf_op jit(solution)/shard_map/wna,wja->wjn/dot_general | solution.py:42
  1015.9 13.2 %fusion.4 = f32[24,24,256]{2,1,0:T(8,128)} fusion(bf16[24,24,2048]{2,0,1:T(8,128)(2,1)} %bitcast.317, bf16[2,24,256,2048]{3,2,1,0:T(8,128)(2,1)} %param.3), kind=kOutput, calls=%fused_computation.4 | convolution fusion | flops 603979776 | bytes 28114944 | tf_op jit(solution)/shard_map/wna,wja->wjn/dot_general | solution.py:50
  1029.0 12.7 %fusion.161 = bf16[1,24,24,256]{3,2,1,0:T(8,128)(2,1)S(1)} fusion(f32[24,24,256]{2,1,0:T(8,128)} %fusion.6, bf16[24,24,2048]{2,0,1:T(8,128)(2,1)} %bitcast.318, bf16[2,24,256,2048]{3,2,1,0:T(8,128)(2,1)} %param.3), kind=kOutput, calls=%fused_computation.113 | convolution fusion | flops 604274688 | bytes 28409856 | tf_op jit(solution)/shard_map/wna,wja->wjn/dot_general | solution.py:40
  1041.8 13.3 %fusion.156 = bf16[1,24,24,256]{3,2,1,0:T(8,128)(2,1)} fusion(f32[24,24,256]{2,1,0:T(8,128)} %fusion.4, bf16[24,24,2048]{2,0,1:T(8,128)(2,1)} %bitcast.312, bf16[2,24,256,2048]{3,2,1,0:T(8,128)(2,1)} %param.3), kind=kOutput, calls=%fused_computation.112 | convolution fusion | flops 604274688 | bytes 28409856 | tf_op jit(solution)/shard_map/wna,wja->wjn/dot_general | solution.py:48
  1056.2 18.3 %all_to_all.189 = bf16[2,24,24,256]{3,1,0,2:T(8,128)(2,1)S(1)} all-to-all(bf16[2,24,24,256]{3,1,0,2:T(8,128)(2,1)S(1)} %copy.259), channel_id=1, replica_groups=mesh['freq'=4,'rcv'=8] {'freq'}, dimensions={2} | all-to-all | bytes 1179648 | tf_op jit(solution)/shard_map/all_to_all | solution.py:79
  1087.9 17.8 %all_to_all.190 = bf16[2,96,6,256]{3,0,2,1:T(2,128)(2,1)S(1)} all-to-all(bf16[2,96,6,256]{3,0,2,1:T(2,128)(2,1)S(1)} %copy.263), channel_id=1, replica_groups=mesh['freq'=4,'rcv'=8] {'freq'}, dimensions={1} | all-to-all | bytes 1179648 | tf_op jit(solution)/shard_map/all_to_all | solution.py:85
  1105.9 12.3 fusion
  1118.2 9.9 fusion.2
  1128.1 12.7 %fusion.75 = bf16[1,24,24,2048]{3,2,1,0:T(8,128)(2,1)} fusion(f32[24,24,2048]{2,1,0:T(8,128)} %fusion, bf16[24,24,256]{2,0,1:T(8,128)(2,1)S(1)} %bitcast.304, bf16[2,24,256,2048]{3,2,1,0:T(8,128)(2,1)} %param.3), kind=kOutput, calls=%fused_computation.69 | convolution fusion | flops 606339072 | bytes 32538624 | tf_op jit(solution)/shard_map/gmk,gim->gik/dot_general | solution.py:67
  1140.8 11.6 fusion.72
  1157.4 52.2 %reduce-scatter.8.cloned.1.call-done = bf16[2,24,24,256]{3,2,1,0:T(8,128)(2,1)} async-done(((bf16[2,24,24,2048]{3,2,1,0:T(8,128)(2,1)}), bf16[2,24,24,256]{3,2,1,0:T(8,128)(2,1)}) %reduce-scatter.8.cloned.1.call-update) | async-done | bytes 589840 | tf_op jit(solution)/shard_map/reduce_scatter | solution.py:87
  1210.8 20.6 %all_to_all.191 = bf16[2,24,24,256]{3,1,0,2:T(8,128)(2,1)S(1)} all-to-all(bf16[2,24,24,256]{3,1,0,2:T(8,128)(2,1)S(1)} %copy.271), channel_id=1, replica_groups=mesh['freq'=4,'rcv'=8] {'freq'}, dimensions={2} | all-to-all | bytes 1179648 | tf_op jit(solution)/shard_map/all_to_all | solution.py:90
  (115 shorter events, 117.1 us)
Async XLA Ops:
  7.2 6.0 copy-start
  7.2 53.4 %all-gather.4.cloned.1.call-start = ((), (), s32[]{:S(2)}) async-start(), calls=%async_computation.15 | async-start | bytes 5308416 | tf_op jit(solution)/shard_map/all_gather | solution.py:76
  17.9 374.2 %reduce-scatter.4.cloned.1.call-start = ((), (), s32[]{:S(2)}) async-start(), calls=%async_computation.16 | async-start | bytes 5308416 | tf_op jit(solution)/shard_map/reduce_scatter | solution.py:87
  257.1 2.3 copy-start.5
  288.5 12.3 copy-start.2
  339.9 125.9 %all-gather.6.cloned.1.call-start = ((), (), s32[]{:S(2)}) async-start(), calls=%async_computation.17 | async-start | bytes 5308416 | tf_op jit(solution)/shard_map/all_gather | solution.py:76
  427.8 373.2 %reduce-scatter.6.cloned.1.call-start = ((), (), s32[]{:S(2)}) async-start(), calls=%async_computation.18 | async-start | bytes 5308416 | tf_op jit(solution)/shard_map/reduce_scatter | solution.py:87
  697.3 12.3 copy-start.3
  748.8 125.7 %all-gather.8.cloned.1.call-start = ((), (), s32[]{:S(2)}) async-start(), calls=%async_computation.19 | async-start | bytes 5308416 | tf_op jit(solution)/shard_map/all_gather | solution.py:76
  836.5 373.1 %reduce-scatter.8.cloned.1.call-start = ((), (), s32[]{:S(2)}) async-start(), calls=%async_computation.20 | async-start | bytes 5308416 | tf_op jit(solution)/shard_map/reduce_scatter | solution.py:87
  1079.4 7.8 copy-start.1
  1105.9 12.3 copy-start.4
Sparse Core Ops, SparseCore 0:
  18.1 42.4 all-gather.3
  340.1 52.0 reduce-scatter.3
  428.0 37.8 all-gather.5
  748.9 52.0 reduce-scatter.5
  836.6 37.8 all-gather.7
  1157.5 51.9 reduce-scatter.7
where the time goes:
time: 1250 us
  blocking collectives  498 us (40%)
  matrix products  376 us (30%)
  waiting for transfers between devices  274 us (22%)
  local copies, waits for them, and re-layouts  60.1 us (5%)
  other arithmetic  20.7 us (2%)
  between operations  15.3 us (1%)
    all_to_all x3, blocking collectives, forward_image(): lax.all_to_all(collected_rows, 'freq', split_axis=1, concat_axis=2, tiled...  328 us
    reduce_scatter x3, waiting for transfers between devices, adjoint_image(): lax.psum_scatter(partial_sums.astype(jnp.bfloat16), 'rcv', scatter_dimens...  156 us
    all_gather x3, waiting for transfers between devices, forward_image(): collected_rows = lax.all_gather(fourier_spectrum, 'rcv', axis=3, tiled=True)  118 us
    all_to_all x3, blocking collectives, adjoint_image(): lax.all_to_all(reduced_total, 'freq', split_axis=2, concat_axis=1, tiled=...  61.8 us
    all_to_all x3, blocking collectives, forward_image(): lax.all_to_all(image.astype(jnp.bfloat16), 'freq', split_axis=2, concat_a...  54.9 us
    all_to_all x3, blocking collectives, adjoint_image(): lax.all_to_all(fourier_spectrum, 'freq', split_axis=1, concat_axis=2, til...  53.2 us
    dot_general x3, matrix products, forward_block(): jnp.einsum('wna,wja->wjn', reflectivity_real, spectral_imaginary, preferr...  39.8 us
    dot_general x3, matrix products, forward_block(): jnp.einsum('wna,wja->wjn', reflectivity_imaginary, spectral_imaginary, pr...  39.5 us
  transfers between devices with their start and end apart: 6, of which 6 were waited for; matrix products, arithmetic and copies ran while one was open for 0% of the time, Pallas kernels for 0%

commit v1 on v0

v1 whole, which is shorter than its diff:
```python
import functools
import math

import jax
import jax.numpy as jnp
from jax import lax
from jax.experimental import pallas as pl
from jax.experimental.pallas import tpu as pltpu
from jax.sharding import PartitionSpec as P

NF = 96
NT = 512
FLO = 8
ITERS = 3
HIER = False
GROUPS = 1
VMEM = 48 * 1024 * 1024


def tables(bands):
    samples = jnp.arange(NT, dtype=jnp.int32)
    bins = FLO + jnp.arange(NF, dtype=jnp.int32)
    phase = bins[:, None] * samples[None, :] % NT
    angles = phase.astype(jnp.float32) * (2.0 * math.pi / NT)
    both = jnp.stack([jnp.cos(angles), -jnp.sin(angles)])
    return both.reshape(2, bands, NF // bands, NT).astype(jnp.bfloat16)


def forward_kernel(r_ref, g_ref, u_ref):
    parts, half = g_ref.shape[0], g_ref.shape[2] // 2
    g = jnp.concatenate([g_ref[j, 0] for j in range(parts)], axis=1)
    dims = (((1,), (1,)), ((), ()))
    a = lax.dot_general(g, r_ref[0, 0], dims, preferred_element_type=jnp.float32)
    b = lax.dot_general(g, r_ref[1, 0], dims, preferred_element_type=jnp.float32)
    u = jnp.concatenate([a[:half] - b[half:], a[half:] + b[:half]], axis=0)
    u_ref[0] = u.astype(u_ref.dtype)


def adjoint_kernel(r_ref, m_ref, w_ref):
    parts, half, width = w_ref.shape[0], w_ref.shape[2] // 2, w_ref.shape[3]
    m = m_ref[0]
    a = jnp.dot(m, r_ref[0, 0], preferred_element_type=jnp.float32)
    b = jnp.dot(m, r_ref[1, 0], preferred_element_type=jnp.float32)
    w = jnp.concatenate([a[:half] + b[half:], a[half:] - b[:half]], axis=0).astype(w_ref.dtype)
    for j in range(parts):
        w_ref[j, 0] = w[:, j * width:(j + 1) * width]


def multiply(kernel, refl, x, out_parts):
    _, bins, rows_s, cols = refl.shape
    lines, width = x.shape[-2:]
    if out_parts:
        x_spec = pl.BlockSpec((1, lines, width), lambda k: (k, 0, 0))
        o_shape = (out_parts, bins, lines, cols // out_parts)
        o_spec = pl.BlockSpec((out_parts, 1, lines, cols // out_parts), lambda k: (0, k, 0, 0))
    else:
        x_spec = pl.BlockSpec((x.shape[0], 1, lines, width), lambda k: (0, k, 0, 0))
        o_shape = (bins, lines, rows_s)
        o_spec = pl.BlockSpec((1, lines, rows_s), lambda k: (k, 0, 0))
    return pl.pallas_call(
        kernel,
        grid=(bins,),
        in_specs=[pl.BlockSpec((2, 1, rows_s, cols), lambda k: (0, k, 0, 0)), x_spec],
        out_specs=o_spec,
        out_shape=jax.ShapeDtypeStruct(o_shape, jnp.bfloat16),
        compiler_params=pltpu.CompilerParams(vmem_limit_bytes=VMEM),
        cost_estimate=pl.CostEstimate(
            flops=8 * bins * lines * rows_s * cols // 2,
            bytes_accessed=4 * bins * rows_s * cols,
            transcendentals=0,
        ),
    )(refl, x)


def to_bands(field, table, bands):
    spec = jnp.einsum("cbkt,pst->bkcps", table, field.astype(jnp.bfloat16), preferred_element_type=jnp.float32)
    spec = lax.all_to_all(spec.astype(jnp.bfloat16), "freq", split_axis=0, concat_axis=0, tiled=True)
    bands, bins, _, focal, width = spec.shape
    return spec.transpose(1, 2, 0, 3, 4).reshape(bins, 2 * bands * focal, width)


def to_trace(image, table, bands):
    bins, lines, width = image.shape
    spec = image.reshape(bins, 2, bands, lines // (2 * bands), width).transpose(2, 0, 1, 3, 4)
    spec = lax.all_to_all(spec, "freq", split_axis=0, concat_axis=0, tiled=True)
    return (2.0 / NT) * jnp.einsum("cbkt,bkcps->pst", table, spec, preferred_element_type=jnp.float32)


def gather(x, n):
    if not HIER:
        return lax.all_gather(x, "rcv", axis=0)
    same = [[2 * i + c for i in range(n // 2)] for c in range(2)]
    pairs = [[2 * i, 2 * i + 1] for i in range(n // 2)]
    y = lax.all_gather(x, "rcv", axis=0, axis_index_groups=pairs)
    y = lax.all_gather(y, "rcv", axis=0, axis_index_groups=[[2 * i + c for i in range(n // 2)] for c in range(2)])
    return y.reshape((n,) + x.shape)


def scatter(x, n):
    return lax.psum_scatter(x, "rcv", scatter_dimension=0, tiled=True).reshape(x.shape[1:])


def local(bands, parts, reflection, direct, onset_index):
    table = tables(bands)
    samples = jnp.arange(NT, dtype=jnp.int32)
    focal = direct.shape[0]
    cuts = [focal * i // GROUPS for i in range(GROUPS + 1)]
    fields = [direct[a:b] for a, b in zip(cuts, cuts[1:])]
    ons = [onset_index[a:b] for a, b in zip(cuts, cuts[1:])]
    plus, minus = list(fields), list(fields)
    for _ in range(ITERS):
        for i in range(GROUPS):
            inside = samples[None, None, :] < ons[i][:, :, None]
            g = gather(to_bands(plus[i], table, bands), parts)
            u = multiply(forward_kernel, reflection, g, 0)
            minus[i] = jnp.where(inside, to_trace(u, table, bands), 0.0)
        for i in range(GROUPS):
            inside = samples[None, None, :] < ons[i][:, :, None]
            m = to_bands(minus[i], table, bands)
            w = scatter(multiply(adjoint_kernel, reflection, m, parts), parts)
            plus[i] = fields[i] + jnp.where(inside, to_trace(w, table, bands), 0.0)
    if GROUPS == 1:
        return plus[0], minus[0]
    return jnp.concatenate(plus), jnp.concatenate(minus)


def solution(mesh):
    placed = (P(None, "freq", "rcv", None), P("freq", "rcv", None), P("freq", "rcv"))
    return jax.shard_map(
        functools.partial(local, mesh.shape["freq"], mesh.shape["rcv"]),
        mesh=mesh,
        in_specs=placed,
        out_specs=(P("freq", "rcv", None), P("freq", "rcv", None)),
        check_vma=False,
    )
```

time: 1250 us -> 739 us (0.59)
  matrix products: 376 us -> 17 us
  blocking collectives: 498 us -> 215 us
  Pallas kernels: 0 us -> 173 us
  local copies, waits for them, and re-layouts: 60.1 us -> 25.5 us
  other arithmetic: 20.7 us -> 0.89 us
    dot_general x48 -> x8, matrix products: 376 us -> 17 us  [the longest x6 13.8 us: to_bands(): jnp.einsum('cbkt,pst->bkcps', table, field.astype(jnp.bfloat16), preferre...]
    all_to_all x12 -> x11, blocking collectives: 498 us -> 215 us  [the longest x6 112 us: to_bands(): lax.all_to_all(spec.astype(jnp.bfloat16), 'freq', split_axis=0, concat_ax...]
    pallas_call x0 -> x6, Pallas kernels: none -> 173 us  [multiply(): pl.pallas_call(kernel, grid=(bins,), in_specs=[pl.BlockSpec((2, 1, rows_s...]
    all_gather x3 -> x0, local copies, waits for them, and re-layouts: 28.4 us -> none  [forward_image(): collected_rows = lax.all_gather(fourier_spectrum, 'rcv', axis=3, tiled=True)]
    another operation x12 -> x2, other arithmetic: 20.7 us -> 0.88 us  [the longest x3 14.8 us: adjoint_block(): return jnp.stack([real_part, imag_part])]
    slice x36 -> x0, local copies, waits for them, and re-layouts: 17.7 us -> none  [the longest x9 17 us: forward_block(): spectral_real, spectral_imaginary = (spectra[0], spectra[1])]
    all_to_all x0 -> x1, waiting for transfers between devices: none -> 16.3 us  [to_trace(): spec = lax.all_to_all(spec, 'freq', split_axis=0, concat_axis=0, tiled=True)]
    unnamed x12 -> x18, local copies, waits for them, and re-layouts: 0.03 us -> 13.4 us
  transfers between devices with their start and end apart: 6 -> 7, of which waited for: 6 -> 7; matrix products, arithmetic and copies ran while one was open for 0% -> 0% of each run, Pallas kernels for 0% -> 0%
where the time goes in v1:
time: 739 us; the launch traced here: 736 us
  waiting for transfers between devices  285 us (39%)
  blocking collectives  215 us (29%)
  Pallas kernels  173 us (23%)
  local copies, waits for them, and re-layouts  25.5 us (3%)
  matrix products  17 us (2%)
  between operations  14.4 us (2%)
    pallas_call x6, Pallas kernels, multiply(): pl.pallas_call(kernel, grid=(bins,), in_specs=[pl.BlockSpec((2, 1, rows_s...  173 us
    reduce_scatter x3, waiting for transfers between devices, scatter(): lax.psum_scatter(x, 'rcv', scatter_dimension=0, tiled=True)  156 us
    all_gather x3, waiting for transfers between devices, gather(): return lax.all_gather(x, 'rcv', axis=0)  112 us
    all_to_all x6, blocking collectives, to_bands(): lax.all_to_all(spec.astype(jnp.bfloat16), 'freq', split_axis=0, concat_ax...  112 us
    all_to_all x5, blocking collectives, to_trace(): spec = lax.all_to_all(spec, 'freq', split_axis=0, concat_axis=0, tiled=True)  103 us
    all_to_all x1, waiting for transfers between devices, to_trace(): spec = lax.all_to_all(spec, 'freq', split_axis=0, concat_axis=0, tiled=True)  16.3 us
  transfers between devices with their start and end apart: 7, of which 7 were waited for; matrix products, arithmetic and copies ran while one was open for 0% of the time, Pallas kernels for 0%

profile of v1, /device:TPU:0, one launch (start us, length us, event | category | flops | bytes accessed | tf_op | source)
XLA Modules:
  0.0 736.0 jit_solution(11415002445813146853)
XLA Ops:
  7.2 0.9 cosine_convert_fusion
  8.1 2.6 fusion.60
  10.7 22.0 %all_to_all.60 = bf16[4,24,2,6,256]{4,1,3,2,0:T(8,128)(2,1)S(1)} all-to-all(bf16[4,24,2,6,256]{4,1,3,2,0:T(8,128)(2,1)S(1)} %copy.36), channel_id=1, replica_groups=mesh['freq'=4,'rcv'=8] {'freq'}, dimensions={0} | all-to-all | bytes 1179648 | tf_op jit(solution)/shard_map/all_to_all | solution.py:77
  32.8 0.9 copy.38
  33.7 38.2 %all-gather.4.cloned.1.call-done.g_ref = bf16[8,24,48,256]{3,2,1,0:T(8,128)(2,1)} async-done(((bf16[1,24,48,256]{3,2,1,0:T(8,128)(2,1)}), bf16[8,24,48,256]{3,2,1,0:T(8,128)(2,1)}) %all-gather.4.cloned.1.call-update) | async-done | bytes 4718608 | tf_op jit(solution)/shard_map/all_gather | solution.py:91
  71.9 2.3 copy-done.5
  74.2 30.4 %shard_map.50 = bf16[24,48,256]{2,1,0:T(8,128)(2,1)S(1)} custom-call(bf16[2,24,256,2048]{3,2,1,0:T(8,128)(2,1)} %r_ref.11, bf16[8,24,48,256]{3,2,1,0:T(8,128)(2,1)S(1)} %copy-done.5), custom_call_target="tpu_custom_call" | custom-call | flops 2415919104 | bytes 50331648 | tf_op jit(solution)/shard_map/pallas_call | solution.py:60
  104.8 0.9 copy.40
  105.6 4.6 all-to-all-start.1
  110.3 16.3 %all-to-all-done.1 = bf16[4,24,2,6,256]{4,1,3,2,0:T(8,128)(2,1)S(1)} async-done(((bf16[4,24,2,6,256]{4,1,3,2,0:T(8,128)(2,1)}), bf16[4,24,2,6,256]{4,1,3,2,0:T(8,128)(2,1)S(1)}, u32[]{:S(2)}, u32[]{:S(2)}) %all-to-all-start.1) | async-done | bytes 589856 | tf_op jit(solution)/shard_map/all_to_all | solution.py:85
  126.6 1.1 fusion.57
  127.8 17.9 %all_to_all.61 = bf16[4,24,2,6,256]{4,1,2,3,0:T(8,128)(2,1)S(1)} all-to-all(bf16[4,24,2,6,256]{4,1,2,3,0:T(8,128)(2,1)S(1)} %copy.42), channel_id=1, replica_groups=mesh['freq'=4,'rcv'=8] {'freq'}, dimensions={0} | all-to-all | bytes 1179648 | tf_op jit(solution)/shard_map/all_to_all | solution.py:77
  145.8 27.5 %shard_map.51 = bf16[8,24,48,256]{3,2,1,0:T(8,128)(2,1)S(1)} custom-call(bf16[2,24,256,2048]{3,2,1,0:T(8,128)(2,1)} %r_ref.11, bf16[24,48,256]{2,1,0:T(8,128)(2,1)S(1)} %copy.44.m_ref), custom_call_target="tpu_custom_call" | custom-call | flops 2415919104 | bytes 50331648 | tf_op jit(solution)/shard_map/pallas_call | solution.py:60
  173.3 2.1 copy-done
  175.5 52.1 %reduce-scatter.4.cloned.1.call-done = bf16[1,24,48,256]{3,2,1,0:T(8,128)(2,1)} async-done(((bf16[8,24,48,256]{3,2,1,0:T(8,128)(2,1)}), bf16[1,24,48,256]{3,2,1,0:T(8,128)(2,1)}) %reduce-scatter.4.cloned.1.call-update) | async-done | bytes 589840 | tf_op jit(solution)/shard_map/reduce_scatter | solution.py:100
  227.6 1.2 copy.45
  228.9 20.4 %all_to_all.62 = bf16[4,24,2,6,256]{4,1,3,2,0:T(8,128)(2,1)} all-to-all(bf16[4,24,2,6,256]{4,1,3,2,0:T(8,128)(2,1)S(1)} %copy.46), channel_id=1, replica_groups=mesh['freq'=4,'rcv'=8] {'freq'}, dimensions={0} | all-to-all | bytes 1179648 | tf_op jit(solution)/shard_map/all_to_all | solution.py:85
  249.3 3.2 fusion.54
  252.5 1.1 copy.48
  253.6 17.7 %all_to_all.63 = bf16[4,24,2,6,256]{4,1,2,3,0:T(8,128)(2,1)S(1)} all-to-all(bf16[4,24,2,6,256]{4,1,2,3,0:T(8,128)(2,1)S(1)} %copy.48), channel_id=1, replica_groups=mesh['freq'=4,'rcv'=8] {'freq'}, dimensions={0} | all-to-all | bytes 1179648 | tf_op jit(solution)/shard_map/all_to_all | solution.py:77
  271.4 0.9 copy.50
  272.4 37.1 %all-gather.6.cloned.1.call-done.g_ref = bf16[8,24,48,256]{3,2,1,0:T(8,128)(2,1)} async-done(((bf16[1,24,48,256]{3,2,1,0:T(8,128)(2,1)}), bf16[8,24,48,256]{3,2,1,0:T(8,128)(2,1)}) %all-gather.6.cloned.1.call-update) | async-done | bytes 4718608 | tf_op jit(solution)/shard_map/all_gather | solution.py:91
  309.5 2.3 copy-done.3
  311.8 30.4 %shard_map.52 = bf16[24,48,256]{2,1,0:T(8,128)(2,1)S(1)} custom-call(bf16[2,24,256,2048]{3,2,1,0:T(8,128)(2,1)} %r_ref.11, bf16[8,24,48,256]{3,2,1,0:T(8,128)(2,1)S(1)} %copy-done.3), custom_call_target="tpu_custom_call" | custom-call | flops 2415919104 | bytes 50331648 | tf_op jit(solution)/shard_map/pallas_call | solution.py:60
  342.4 20.8 %all_to_all.64 = bf16[4,24,2,6,256]{4,1,3,2,0:T(8,128)(2,1)} all-to-all(bf16[4,24,2,6,256]{4,1,3,2,0:T(8,128)(2,1)S(1)} %copy.52), channel_id=1, replica_groups=mesh['freq'=4,'rcv'=8] {'freq'}, dimensions={0} | all-to-all | bytes 1179648 | tf_op jit(solution)/shard_map/all_to_all | solution.py:85
  363.3 3.0 fusion.51
  366.3 1.1 copy.54
  367.4 18.3 %all_to_all.65 = bf16[4,24,2,6,256]{4,1,2,3,0:T(8,128)(2,1)S(1)} all-to-all(bf16[4,24,2,6,256]{4,1,2,3,0:T(8,128)(2,1)S(1)} %copy.54), channel_id=1, replica_groups=mesh['freq'=4,'rcv'=8] {'freq'}, dimensions={0} | all-to-all | bytes 1179648 | tf_op jit(solution)/shard_map/all_to_all | solution.py:77
  385.9 27.5 %shard_map.53 = bf16[8,24,48,256]{3,2,1,0:T(8,128)(2,1)S(1)} custom-call(bf16[2,24,256,2048]{3,2,1,0:T(8,128)(2,1)} %r_ref.11, bf16[24,48,256]{2,1,0:T(8,128)(2,1)S(1)} %copy.56.m_ref), custom_call_target="tpu_custom_call" | custom-call | flops 2415919104 | bytes 50331648 | tf_op jit(solution)/shard_map/pallas_call | solution.py:60
  413.4 2.1 copy-done.1
  415.6 52.1 %reduce-scatter.6.cloned.1.call-done = bf16[1,24,48,256]{3,2,1,0:T(8,128)(2,1)} async-done(((bf16[8,24,48,256]{3,2,1,0:T(8,128)(2,1)}), bf16[1,24,48,256]{3,2,1,0:T(8,128)(2,1)}) %reduce-scatter.6.cloned.1.call-update) | async-done | bytes 589840 | tf_op jit(solution)/shard_map/reduce_scatter | solution.py:100
  467.7 1.2 copy.57
  469.0 20.4 %all_to_all.66 = bf16[4,24,2,6,256]{4,1,3,2,0:T(8,128)(2,1)} all-to-all(bf16[4,24,2,6,256]{4,1,3,2,0:T(8,128)(2,1)S(1)} %copy.58), channel_id=1, replica_groups=mesh['freq'=4,'rcv'=8] {'freq'}, dimensions={0} | all-to-all | bytes 1179648 | tf_op jit(solution)/shard_map/all_to_all | solution.py:85
  489.4 3.2 fusion.48
  492.6 1.1 copy.60
  493.7 17.7 %all_to_all.67 = bf16[4,24,2,6,256]{4,1,2,3,0:T(8,128)(2,1)S(1)} all-to-all(bf16[4,24,2,6,256]{4,1,2,3,0:T(8,128)(2,1)S(1)} %copy.60), channel_id=1, replica_groups=mesh['freq'=4,'rcv'=8] {'freq'}, dimensions={0} | all-to-all | bytes 1179648 | tf_op jit(solution)/shard_map/all_to_all | solution.py:77
  511.4 0.9 copy.62
  512.4 37.1 %all-gather.8.cloned.1.call-done.g_ref = bf16[8,24,48,256]{3,2,1,0:T(8,128)(2,1)} async-done(((bf16[1,24,48,256]{3,2,1,0:T(8,128)(2,1)}), bf16[8,24,48,256]{3,2,1,0:T(8,128)(2,1)}) %all-gather.8.cloned.1.call-update) | async-done | bytes 4718608 | tf_op jit(solution)/shard_map/all_gather | solution.py:91
  549.6 2.3 copy-done.4
  551.9 30.4 %shard_map.54 = bf16[24,48,256]{2,1,0:T(8,128)(2,1)S(1)} custom-call(bf16[2,24,256,2048]{3,2,1,0:T(8,128)(2,1)} %r_ref.11, bf16[8,24,48,256]{3,2,1,0:T(8,128)(2,1)S(1)} %copy-done.4), custom_call_target="tpu_custom_call" | custom-call | flops 2415919104 | bytes 50331648 | tf_op jit(solution)/shard_map/pallas_call | solution.py:60
  582.5 20.7 %all_to_all.68 = bf16[4,24,2,6,256]{4,1,2,3,0:T(8,128)(2,1)S(1)} all-to-all(bf16[4,24,2,6,256]{4,1,2,3,0:T(8,128)(2,1)S(1)} %copy.64), channel_id=1, replica_groups=mesh['freq'=4,'rcv'=8] {'freq'}, dimensions={0} | all-to-all | bytes 1179648 | tf_op jit(solution)/shard_map/all_to_all | solution.py:85
  604.7 18.3 %all_to_all.69 = bf16[4,24,2,6,256]{4,1,2,3,0:T(8,128)(2,1)S(1)} all-to-all(bf16[4,24,2,6,256]{4,1,2,3,0:T(8,128)(2,1)S(1)} %copy.66), channel_id=1, replica_groups=mesh['freq'=4,'rcv'=8] {'freq'}, dimensions={0} | all-to-all | bytes 1179648 | tf_op jit(solution)/shard_map/all_to_all | solution.py:77
  623.2 27.5 %shard_map.55 = bf16[8,24,48,256]{3,2,1,0:T(8,128)(2,1)S(1)} custom-call(bf16[2,24,256,2048]{3,2,1,0:T(8,128)(2,1)} %r_ref.11, bf16[24,48,256]{2,1,0:T(8,128)(2,1)S(1)} %copy.68.m_ref), custom_call_target="tpu_custom_call" | custom-call | flops 2415919104 | bytes 50331648 | tf_op jit(solution)/shard_map/pallas_call | solution.py:60
  650.7 2.1 copy-done.2
  652.8 52.2 %reduce-scatter.8.cloned.1.call-done = bf16[1,24,48,256]{3,2,1,0:T(8,128)(2,1)} async-done(((bf16[8,24,48,256]{3,2,1,0:T(8,128)(2,1)}), bf16[1,24,48,256]{3,2,1,0:T(8,128)(2,1)}) %reduce-scatter.8.cloned.1.call-update) | async-done | bytes 589840 | tf_op jit(solution)/shard_map/reduce_scatter | solution.py:100
  705.0 1.2 copy.69
  706.3 20.3 %all_to_all.70 = bf16[4,24,2,6,256]{4,1,2,3,0:T(8,128)(2,1)S(1)} all-to-all(bf16[4,24,2,6,256]{4,1,2,3,0:T(8,128)(2,1)S(1)} %copy.70), channel_id=1, replica_groups=mesh['freq'=4,'rcv'=8] {'freq'}, dimensions={0} | all-to-all | bytes 1179648 | tf_op jit(solution)/shard_map/all_to_all | solution.py:85
  726.6 2.5 fusion.1
  (48 shorter events, 3.2 us)
Async XLA Ops:
  7.2 64.7 %all-gather.4.cloned.1.call-start = ((), (), s32[]{:S(2)}) async-start(), calls=%async_computation.15 | async-start | bytes 5308416 | tf_op jit(solution)/shard_map/all_gather | solution.py:91
  71.9 2.3 copy-start.5
  104.6 22.0 %copy-start.8 = (s32[6,256]{1,0:T(8,128)S(1)}, s32[6,256]{1,0:T(8,128)}, u32[]{:S(2)}) copy-start(s32[6,256]{1,0:T(8,128)} %param.5) | copy-start | bytes 18436
  105.6 20.9 %all-to-all-start.1 = ((bf16[4,24,2,6,256]{4,1,3,2,0:T(8,128)(2,1)}), bf16[4,24,2,6,256]{4,1,3,2,0:T(8,128)(2,1)S(1)}, u32[]{:S(2)}, u32[]{:S(2)}) async-start(bf16[4,24,2,6,256]{4,1,3,2,0:T(8,128)(2,1)} %copy.40), calls=%async_computation.1 | async-start | bytes 1179648 | tf_op jit(solution)/shard_map/all_to_all | solution.py:85
  110.2 117.3 %reduce-scatter.4.cloned.1.call-start = ((), (), s32[]{:S(2)}) async-start(), calls=%async_computation.16 | async-start | bytes 5308416 | tf_op jit(solution)/shard_map/reduce_scatter | solution.py:100
  173.3 2.1 copy-start
  175.4 73.9 %copy-start.6 = (f32[6,256,512]{2,1,0:T(8,128)S(1)}, f32[6,256,512]{2,1,0:T(8,128)}, u32[]{:S(2)}) copy-start(f32[6,256,512]{2,1,0:T(8,128)} %param.4) | copy-start | bytes 9437188
  175.4 134.1 %all-gather.6.cloned.1.call-start = ((), (), s32[]{:S(2)}) async-start(), calls=%async_computation.17 | async-start | bytes 5308416 | tf_op jit(solution)/shard_map/all_gather | solution.py:91
  272.3 195.4 %reduce-scatter.6.cloned.1.call-start = ((), (), s32[]{:S(2)}) async-start(), calls=%async_computation.18 | async-start | bytes 5308416 | tf_op jit(solution)/shard_map/reduce_scatter | solution.py:100
  309.5 2.3 copy-start.3
  413.4 2.1 copy-start.1
  415.5 134.1 %all-gather.8.cloned.1.call-start = ((), (), s32[]{:S(2)}) async-start(), calls=%async_computation.19 | async-start | bytes 5308416 | tf_op jit(solution)/shard_map/all_gather | solution.py:91
  512.4 192.6 %reduce-scatter.8.cloned.1.call-start = ((), (), s32[]{:S(2)}) async-start(), calls=%async_computation.20 | async-start | bytes 5308416 | tf_op jit(solution)/shard_map/reduce_scatter | solution.py:100
  549.6 2.3 copy-start.4
  604.0 19.1 %copy-start.7 = (f32[6,256,512]{2,1,0:T(8,128)}, f32[6,256,512]{2,1,0:T(8,128)S(1)}, u32[]{:S(2)}) copy-start(f32[6,256,512]{2,1,0:T(8,128)S(1)} %fusion.2) | copy-start | bytes 9437188
  650.7 2.1 copy-start.2
Sparse Core Ops, SparseCore 0:
  33.8 38.0 all-gather.3
  175.5 52.0 reduce-scatter.3
  272.4 37.0 all-gather.5
  415.6 52.0 reduce-scatter.5
  512.5 37.0 all-gather.7
  653.0 52.0 reduce-scatter.7

commit v2 on v1

--- a/solution.py
+++ b/solution.py
@@ -12,7 +12,6 @@
 NT = 512
 FLO = 8
 ITERS = 3
-HIER = False
 GROUPS = 1
 VMEM = 48 * 1024 * 1024
 
@@ -30,8 +29,8 @@
     parts, half = g_ref.shape[0], g_ref.shape[2] // 2
     g = jnp.concatenate([g_ref[j, 0] for j in range(parts)], axis=1)
     dims = (((1,), (1,)), ((), ()))
-    a = lax.dot_general(g, r_ref[0, 0], dims, preferred_element_type=jnp.float32)
-    b = lax.dot_general(g, r_ref[1, 0], dims, preferred_element_type=jnp.float32)
+    a = lax.dot_general(r_ref[0, 0], g, dims, preferred_element_type=jnp.float32).T
+    b = lax.dot_general(r_ref[1, 0], g, dims, preferred_element_type=jnp.float32).T
     u = jnp.concatenate([a[:half] - b[half:], a[half:] + b[:half]], axis=0)
     u_ref[0] = u.astype(u_ref.dtype)
 
@@ -72,32 +71,179 @@
     )(refl, x)
 
 
+def exchange_kernel(n, x_ref, o_ref, send_sem, recv_sem, own_sem):
+    me = lax.axis_index("freq")
+    barrier = pltpu.get_barrier_semaphore()
+    for d in range(1, n):
+        pl.semaphore_signal(
+            barrier, inc=1, device_id={"freq": lax.rem(me + d, n)}, device_id_type=pl.DeviceIdType.MESH
+        )
+    pl.semaphore_wait(barrier, n - 1)
+    copies = []
+    for d in range(1, n):
+        to = lax.rem(me + d, n)
+        copies.append(
+            pltpu.make_async_remote_copy(
+                src_ref=x_ref.at[to],
+                dst_ref=o_ref.at[me],
+                send_sem=send_sem.at[d - 1],
+                recv_sem=recv_sem.at[d - 1],
+                device_id={"freq": to},
+                device_id_type=pl.DeviceIdType.MESH,
+            )
+        )
+    copies.append(pltpu.make_async_copy(x_ref.at[me], o_ref.at[me], own_sem))
+    for copy in copies:
+        copy.start()
+    for copy in copies:
+        copy.wait()
+
+
+def exchange(x):
+    n = x.shape[0]
+    return pl.pallas_call(
+        functools.partial(exchange_kernel, n),
+        out_shape=jax.ShapeDtypeStruct(x.shape, x.dtype),
+        in_specs=[pl.BlockSpec(memory_space=pltpu.VMEM)],
+        out_specs=pl.BlockSpec(memory_space=pltpu.VMEM),
+        scratch_shapes=[
+            pltpu.SemaphoreType.DMA((n - 1,)),
+            pltpu.SemaphoreType.DMA((n - 1,)),
+            pltpu.SemaphoreType.DMA,
+        ],
+        compiler_params=pltpu.CompilerParams(collective_id=0, has_side_effects=True, vmem_limit_bytes=16 * 1024 * 1024),
+    )(x)
+
+
 def to_bands(field, table, bands):
-    spec = jnp.einsum("cbkt,pst->bkcps", table, field.astype(jnp.bfloat16), preferred_element_type=jnp.float32)
-    spec = lax.all_to_all(spec.astype(jnp.bfloat16), "freq", split_axis=0, concat_axis=0, tiled=True)
-    bands, bins, _, focal, width = spec.shape
-    return spec.transpose(1, 2, 0, 3, 4).reshape(bins, 2 * bands * focal, width)
+    spec = jnp.einsum("cbkt,pst->bcpks", table, field.astype(jnp.bfloat16), preferred_element_type=jnp.float32)
+    _, _, focal, bins, width = spec.shape
+    spec = exchange(spec.astype(jnp.bfloat16).reshape(bands, -1, width))
+    spec = spec.reshape(bands, 2, focal, bins, width)
+    return spec.transpose(3, 1, 0, 2, 4).reshape(bins, 2 * bands * focal, width)
 
 
 def to_trace(image, table, bands):
     bins, lines, width = image.shape
-    spec = image.reshape(bins, 2, bands, lines // (2 * bands), width).transpose(2, 0, 1, 3, 4)
-    spec = lax.all_to_all(spec, "freq", split_axis=0, concat_axis=0, tiled=True)
-    return (2.0 / NT) * jnp.einsum("cbkt,bkcps->pst", table, spec, preferred_element_type=jnp.float32)
+    focal = lines // (2 * bands)
+    spec = image.reshape(bins, 2, bands, focal, width).transpose(2, 1, 3, 0, 4)
+    spec = exchange(spec.reshape(bands, -1, width)).reshape(bands, 2, focal, bins, width)
+    return (2.0 / NT) * jnp.einsum("cbkt,bcpks->pst", table, spec, preferred_element_type=jnp.float32)
+
+
+def reach(rows, axis_device):
+    barrier = pltpu.get_barrier_semaphore()
+    for to in axis_device:
+        pl.semaphore_signal(barrier, inc=1, device_id={"rcv": to}, device_id_type=pl.DeviceIdType.MESH)
+    pl.semaphore_wait(barrier, rows)
+
+
+def remote(src, dst, send_sem, recv_sem, to):
+    return pltpu.make_async_remote_copy(
+        src_ref=src, dst_ref=dst, send_sem=send_sem, recv_sem=recv_sem,
+        device_id={"rcv": to}, device_id_type=pl.DeviceIdType.MESH,
+    )
+
+
+def gather_kernel(n, x_ref, o_ref, send_sem, recv_sem, own_sem):
+    me, chips = lax.axis_index("rcv"), n // 2
+    chip, core = me // 2, lax.rem(me, 2)
+    sibling = 2 * chip + 1 - core
+    peers = [2 * lax.rem(chip + d, chips) + core for d in range(1, chips)]
+    reach(chips, peers + [sibling])
+    direct = []
+    for i, to in enumerate(peers + [sibling]):
+        direct.append(remote(x_ref, o_ref.at[me], send_sem.at[i], recv_sem.at[i], to))
+        direct[-1].start()
+    own = pltpu.make_async_copy(x_ref, o_ref.at[me], own_sem)
+    own.start()
+    passed = []
+    for d in range(1, chips):
+        direct[d - 1].wait_recv()
+        slot = 2 * lax.rem(chip - d + chips, chips) + core
+        at = chips - 1 + d
+        passed.append(remote(o_ref.at[slot], o_ref.at[slot], send_sem.at[at], recv_sem.at[at], sibling))
+        passed[-1].start()
+    direct[-1].wait_recv()
+    for copy in direct:
+        copy.wait_send()
+    for copy in passed:
+        copy.wait()
+    own.wait()
+
+
+def scatter_kernel(n, x_ref, o_ref, pair, held, landed, total, pair_send, pair_recv, send_sem, recv_sem):
+    me, chips = lax.axis_index("rcv"), n // 2
+    chip, core = me // 2, lax.rem(me, 2)
+    sibling = 2 * chip + 1 - core
+    bins = o_ref.shape[0]
+    targets = [lax.rem(chip + d, chips) for d in range(1, chips + 1)]
+    reach(chips, [2 * to + core for to in targets[:-1]] + [sibling])
+    across = []
+    for i, to in enumerate(targets):
+        across.append(remote(x_ref.at[2 * to + 1 - core], pair.at[i], pair_send.at[i], pair_recv.at[i], sibling))
+        across[-1].start()
+    sent = []
+    for i, to in enumerate(targets):
+        across[i].wait_recv()
+        last = i == chips - 1
+
+        def add(k, carry, i=i, to=to, last=last):
+            value = x_ref[2 * to + core, k].astype(jnp.float32) + pair[i, k].astype(jnp.float32)
+            if last:
+                total[k] = value
+            else:
+                held[i, k] = value.astype(held.dtype)
+            return carry
+
+        lax.fori_loop(0, bins, add, 0)
+        if not last:
+            sent.append(remote(held.at[i], landed.at[i], send_sem.at[i], recv_sem.at[i], 2 * to + core))
+            sent[-1].start()
+    for copy in sent:
+        copy.wait_recv()
+
+    def finish(k, carry):
+        value = total[k]
+        for i in range(chips - 1):
+            value = value + landed[i, k].astype(jnp.float32)
+        o_ref[k] = value.astype(o_ref.dtype)
+        return carry
+
+    lax.fori_loop(0, bins, finish, 0)
+    for copy in sent + across:
+        copy.wait_send()
 
 
 def gather(x, n):
-    if not HIER:
-        return lax.all_gather(x, "rcv", axis=0)
-    same = [[2 * i + c for i in range(n // 2)] for c in range(2)]
-    pairs = [[2 * i, 2 * i + 1] for i in range(n // 2)]
-    y = lax.all_gather(x, "rcv", axis=0, axis_index_groups=pairs)
-    y = lax.all_gather(y, "rcv", axis=0, axis_index_groups=[[2 * i + c for i in range(n // 2)] for c in range(2)])
-    return y.reshape((n,) + x.shape)
+    sems = pltpu.SemaphoreType.DMA((n - 1,))
+    return pl.pallas_call(
+        functools.partial(gather_kernel, n),
+        out_shape=jax.ShapeDtypeStruct((n,) + x.shape, x.dtype),
+        in_specs=[pl.BlockSpec(memory_space=pltpu.VMEM)],
+        out_specs=pl.BlockSpec(memory_space=pltpu.VMEM),
+        scratch_shapes=[sems, sems, pltpu.SemaphoreType.DMA],
+        compiler_params=pltpu.CompilerParams(collective_id=1, has_side_effects=True, vmem_limit_bytes=24 * 1024 * 1024),
+    )(x)
 
 
 def scatter(x, n):
-    return lax.psum_scatter(x, "rcv", scatter_dimension=0, tiled=True).reshape(x.shape[1:])
+    block = x.shape[1:]
+    whole, rest = pltpu.SemaphoreType.DMA((n // 2,)), pltpu.SemaphoreType.DMA((n // 2 - 1,))
+    return pl.pallas_call(
+        functools.partial(scatter_kernel, n),
+        out_shape=jax.ShapeDtypeStruct(block, x.dtype),
+        in_specs=[pl.BlockSpec(memory_space=pltpu.VMEM)],
+        out_specs=pl.BlockSpec(memory_space=pltpu.VMEM),
+        scratch_shapes=[
+            pltpu.VMEM((n // 2,) + block, x.dtype),
+            pltpu.VMEM((n // 2 - 1,) + block, x.dtype),
+            pltpu.VMEM((n // 2 - 1,) + block, x.dtype),
+            pltpu.VMEM(block, jnp.float32),
+            whole, whole, rest, rest,
+        ],
+        compiler_params=pltpu.CompilerParams(collective_id=2, has_side_effects=True, vmem_limit_bytes=32 * 1024 * 1024),
+    )(x)
 
 
 def local(bands, parts, reflection, direct, onset_index):

time: 739 us -> 573 us (0.78)
  Pallas kernels: 173 us -> 551 us
  waiting for transfers between devices: 285 us -> 0 us
  blocking collectives: 215 us -> 0 us
  local copies, waits for them, and re-layouts: 25.5 us -> 2.5 us
  between operations: 14.4 us -> 1.15 us
    pallas_call x0 -> x18, Pallas kernels: none -> 377 us  [the longest x12 190 us: exchange(): pl.pallas_call(functools.partial(exchange_kernel, n), out_shape=jax.Shape...]
    all_to_all x11 -> x0, blocking collectives: 215 us -> none  [the longest x6 112 us: to_bands(): lax.all_to_all(spec.astype(jnp.bfloat16), 'freq', split_axis=0, concat_ax...]
    reduce_scatter x3 -> x0, waiting for transfers between devices: 156 us -> none  [scatter(): lax.psum_scatter(x, 'rcv', scatter_dimension=0, tiled=True)]
    all_gather x3 -> x0, waiting for transfers between devices: 112 us -> none  [gather(): return lax.all_gather(x, 'rcv', axis=0)]
    all_to_all x1 -> x0, waiting for transfers between devices: 16.3 us -> none  [to_trace(): spec = lax.all_to_all(spec, 'freq', split_axis=0, concat_axis=0, tiled=True)]
    unnamed x18 -> x6, local copies, waits for them, and re-layouts: 13.4 us -> 0.02 us
  transfers between devices with their start and end apart: 7 -> 0, of which waited for: 7 -> 0; matrix products, arithmetic and copies ran while one was open for 0% -> 0% of each run, Pallas kernels for 0% -> 0%
where the time goes in v2:
time: 573 us; the launch traced here: 571 us
  Pallas kernels  551 us (96%)
  matrix products  15.1 us (3%)
    pallas_call x12, Pallas kernels, exchange(): pl.pallas_call(functools.partial(exchange_kernel, n), out_shape=jax.Shape...  190 us
    pallas_call x6, Pallas kernels, multiply(): pl.pallas_call(kernel, grid=(bins,), in_specs=[pl.BlockSpec((2, 1, rows_s...  174 us
    pallas_call x3, Pallas kernels, scatter(): pl.pallas_call(functools.partial(scatter_kernel, n), out_shape=jax.ShapeD...  94.6 us
    pallas_call x3, Pallas kernels, gather(): pl.pallas_call(functools.partial(gather_kernel, n), out_shape=jax.ShapeDt...  92.6 us
    dot_general x6, matrix products, to_bands(): jnp.einsum('cbkt,pst->bcpks', table, field.astype(jnp.bfloat16), preferre...  11.9 us

profile of v2, /device:TPU:0, one launch (start us, length us, event | category | flops | bytes accessed | tf_op | source)
XLA Modules:
  0.0 570.7 jit_solution(16180531066229892984)
XLA Ops:
  0.6 0.9 cosine_convert_fusion
  1.5 2.6 fusion.60
  4.1 15.6 %shard_map.50 = bf16[4,288,256]{2,1,0:T(8,128)(2,1)S(1)} custom-call(bf16[4,288,256]{2,1,0:T(8,128)(2,1)S(1)} %bitcast.215), custom_call_target="tpu_custom_call" | custom-call | tf_op jit(solution)/shard_map/pallas_call | solution.py:104
  19.8 0.1 copy.29.x_ref
  19.9 31.4 %shard_map.51.g_ref = bf16[8,24,48,256]{3,2,1,0:T(8,128)(2,1)S(1)} custom-call(bf16[24,48,256]{2,1,0:T(8,128)(2,1)S(1)} %copy.29.x_ref), custom_call_target="tpu_custom_call" | custom-call | tf_op jit(solution)/shard_map/pallas_call | solution.py:220
  51.4 30.5 %shard_map.52 = bf16[24,48,256]{2,1,0:T(8,128)(2,1)S(1)} custom-call(bf16[2,24,256,2048]{3,2,1,0:T(8,128)(2,1)} %r_ref.11, bf16[8,24,48,256]{3,2,1,0:T(8,128)(2,1)S(1)} %shard_map.51.g_ref), custom_call_target="tpu_custom_call" | custom-call | flops 2415919104 | bytes 50331648 | tf_op jit(solution)/shard_map/pallas_call | solution.py:59
  81.9 0.0 copy-start.2
  81.9 0.2 copy.30
  82.1 16.6 %shard_map.53 = bf16[4,288,256]{2,1,0:T(8,128)(2,1)S(1)} custom-call(bf16[4,288,256]{2,1,0:T(8,128)(2,1)S(1)} %bitcast.217), custom_call_target="tpu_custom_call" | custom-call | tf_op jit(solution)/shard_map/pallas_call | solution.py:104
  98.7 1.1 fusion.57
  99.9 15.4 %shard_map.54 = bf16[4,288,256]{2,1,0:T(8,128)(2,1)S(1)} custom-call(bf16[4,288,256]{2,1,0:T(8,128)(2,1)S(1)} %bitcast.218), custom_call_target="tpu_custom_call" | custom-call | tf_op jit(solution)/shard_map/pallas_call | solution.py:104
  115.3 0.1 copy.34.m_ref
  115.5 27.5 %shard_map.55.x_ref = bf16[8,24,48,256]{3,2,1,0:T(8,128)(2,1)S(1)} custom-call(bf16[2,24,256,2048]{3,2,1,0:T(8,128)(2,1)} %r_ref.11, bf16[24,48,256]{2,1,0:T(8,128)(2,1)S(1)} %copy.34.m_ref), custom_call_target="tpu_custom_call" | custom-call | flops 2415919104 | bytes 50331648 | tf_op jit(solution)/shard_map/pallas_call | solution.py:59
  142.9 31.6 %shard_map.56 = bf16[24,48,256]{2,1,0:T(8,128)(2,1)S(1)} custom-call(bf16[8,24,48,256]{3,2,1,0:T(8,128)(2,1)S(1)} %shard_map.55.x_ref), custom_call_target="tpu_custom_call" | custom-call | tf_op jit(solution)/shard_map/pallas_call | solution.py:233
  174.5 0.2 copy.35
  174.7 16.3 %shard_map.57 = bf16[4,288,256]{2,1,0:T(8,128)(2,1)S(1)} custom-call(bf16[4,288,256]{2,1,0:T(8,128)(2,1)S(1)} %bitcast.220), custom_call_target="tpu_custom_call" | custom-call | tf_op jit(solution)/shard_map/pallas_call | solution.py:104
  191.1 3.2 fusion.54
  194.3 14.8 %shard_map.58 = bf16[4,288,256]{2,1,0:T(8,128)(2,1)S(1)} custom-call(bf16[4,288,256]{2,1,0:T(8,128)(2,1)S(1)} %bitcast.221), custom_call_target="tpu_custom_call" | custom-call | tf_op jit(solution)/shard_map/pallas_call | solution.py:104
  209.2 0.1 copy.39.x_ref
  209.3 30.6 %shard_map.59.g_ref = bf16[8,24,48,256]{3,2,1,0:T(8,128)(2,1)S(1)} custom-call(bf16[24,48,256]{2,1,0:T(8,128)(2,1)S(1)} %copy.39.x_ref), custom_call_target="tpu_custom_call" | custom-call | tf_op jit(solution)/shard_map/pallas_call | solution.py:220
  239.9 30.5 %shard_map.60 = bf16[24,48,256]{2,1,0:T(8,128)(2,1)S(1)} custom-call(bf16[2,24,256,2048]{3,2,1,0:T(8,128)(2,1)} %r_ref.11, bf16[8,24,48,256]{3,2,1,0:T(8,128)(2,1)S(1)} %shard_map.59.g_ref), custom_call_target="tpu_custom_call" | custom-call | flops 2415919104 | bytes 50331648 | tf_op jit(solution)/shard_map/pallas_call | solution.py:59
  270.4 0.2 copy.40
  270.6 16.6 %shard_map.61 = bf16[4,288,256]{2,1,0:T(8,128)(2,1)S(1)} custom-call(bf16[4,288,256]{2,1,0:T(8,128)(2,1)S(1)} %bitcast.223), custom_call_target="tpu_custom_call" | custom-call | tf_op jit(solution)/shard_map/pallas_call | solution.py:104
  287.2 1.1 fusion.51
  288.4 15.4 %shard_map.62 = bf16[4,288,256]{2,1,0:T(8,128)(2,1)S(1)} custom-call(bf16[4,288,256]{2,1,0:T(8,128)(2,1)S(1)} %bitcast.224), custom_call_target="tpu_custom_call" | custom-call | tf_op jit(solution)/shard_map/pallas_call | solution.py:104
  303.8 0.1 copy.44.m_ref
  304.0 27.5 %shard_map.63.x_ref = bf16[8,24,48,256]{3,2,1,0:T(8,128)(2,1)S(1)} custom-call(bf16[2,24,256,2048]{3,2,1,0:T(8,128)(2,1)} %r_ref.11, bf16[24,48,256]{2,1,0:T(8,128)(2,1)S(1)} %copy.44.m_ref), custom_call_target="tpu_custom_call" | custom-call | flops 2415919104 | bytes 50331648 | tf_op jit(solution)/shard_map/pallas_call | solution.py:59
  331.4 31.5 %shard_map.64 = bf16[24,48,256]{2,1,0:T(8,128)(2,1)S(1)} custom-call(bf16[8,24,48,256]{3,2,1,0:T(8,128)(2,1)S(1)} %shard_map.63.x_ref), custom_call_target="tpu_custom_call" | custom-call | tf_op jit(solution)/shard_map/pallas_call | solution.py:233
  362.9 0.2 copy.45
  363.1 16.3 %shard_map.65 = bf16[4,288,256]{2,1,0:T(8,128)(2,1)S(1)} custom-call(bf16[4,288,256]{2,1,0:T(8,128)(2,1)S(1)} %bitcast.226), custom_call_target="tpu_custom_call" | custom-call | tf_op jit(solution)/shard_map/pallas_call | solution.py:104
  379.4 3.2 fusion.48
  382.7 14.8 %shard_map.66 = bf16[4,288,256]{2,1,0:T(8,128)(2,1)S(1)} custom-call(bf16[4,288,256]{2,1,0:T(8,128)(2,1)S(1)} %bitcast.227), custom_call_target="tpu_custom_call" | custom-call | tf_op jit(solution)/shard_map/pallas_call | solution.py:104
  397.6 0.1 copy.49.x_ref
  397.7 30.6 %shard_map.67.g_ref = bf16[8,24,48,256]{3,2,1,0:T(8,128)(2,1)S(1)} custom-call(bf16[24,48,256]{2,1,0:T(8,128)(2,1)S(1)} %copy.49.x_ref), custom_call_target="tpu_custom_call" | custom-call | tf_op jit(solution)/shard_map/pallas_call | solution.py:220
  428.3 30.5 %shard_map.68 = bf16[24,48,256]{2,1,0:T(8,128)(2,1)S(1)} custom-call(bf16[2,24,256,2048]{3,2,1,0:T(8,128)(2,1)} %r_ref.11, bf16[8,24,48,256]{3,2,1,0:T(8,128)(2,1)S(1)} %shard_map.67.g_ref), custom_call_target="tpu_custom_call" | custom-call | flops 2415919104 | bytes 50331648 | tf_op jit(solution)/shard_map/pallas_call | solution.py:59
  458.8 0.2 copy.50
  459.0 16.6 %shard_map.69 = bf16[4,288,256]{2,1,0:T(8,128)(2,1)S(1)} custom-call(bf16[4,288,256]{2,1,0:T(8,128)(2,1)S(1)} %bitcast.229), custom_call_target="tpu_custom_call" | custom-call | tf_op jit(solution)/shard_map/pallas_call | solution.py:104
  475.7 0.7 fusion.2
  476.4 0.0 copy-start.1
  476.4 0.7 fusion.45
  477.1 15.4 %shard_map.70 = bf16[4,288,256]{2,1,0:T(8,128)(2,1)S(1)} custom-call(bf16[4,288,256]{2,1,0:T(8,128)(2,1)S(1)} %bitcast.230), custom_call_target="tpu_custom_call" | custom-call | tf_op jit(solution)/shard_map/pallas_call | solution.py:104
  492.6 0.1 copy.56.m_ref
  492.7 27.5 %shard_map.71.x_ref = bf16[8,24,48,256]{3,2,1,0:T(8,128)(2,1)S(1)} custom-call(bf16[2,24,256,2048]{3,2,1,0:T(8,128)(2,1)} %r_ref.11, bf16[24,48,256]{2,1,0:T(8,128)(2,1)S(1)} %copy.56.m_ref), custom_call_target="tpu_custom_call" | custom-call | flops 2415919104 | bytes 50331648 | tf_op jit(solution)/shard_map/pallas_call | solution.py:59
  520.2 0.0 copy-start
  520.2 31.5 %shard_map.72 = bf16[24,48,256]{2,1,0:T(8,128)(2,1)S(1)} custom-call(bf16[8,24,48,256]{3,2,1,0:T(8,128)(2,1)S(1)} %shard_map.71.x_ref), custom_call_target="tpu_custom_call" | custom-call | tf_op jit(solution)/shard_map/pallas_call | solution.py:233
  551.7 0.2 copy.57
  552.0 16.2 %shard_map.73 = bf16[4,288,256]{2,1,0:T(8,128)(2,1)S(1)} custom-call(bf16[4,288,256]{2,1,0:T(8,128)(2,1)S(1)} %bitcast.232), custom_call_target="tpu_custom_call" | custom-call | tf_op jit(solution)/shard_map/pallas_call | solution.py:104
  568.2 2.5 fusion.1
  (23 shorter events, 0.8 us)
Async XLA Ops:
  81.9 16.8 %copy-start.2 = (s32[6,256]{1,0:T(8,128)S(1)}, s32[6,256]{1,0:T(8,128)}, u32[]{:S(2)}) copy-start(s32[6,256]{1,0:T(8,128)} %param.5) | copy-start | bytes 18436
  476.4 16.1 %copy-start.1 = (f32[6,256,512]{2,1,0:T(8,128)}, f32[6,256,512]{2,1,0:T(8,128)S(1)}, u32[]{:S(2)}) copy-start(f32[6,256,512]{2,1,0:T(8,128)S(1)} %fusion.2) | copy-start | bytes 9437188
  520.2 48.0 %copy-start = (f32[6,256,512]{2,1,0:T(8,128)S(1)}, f32[6,256,512]{2,1,0:T(8,128)}, u32[]{:S(2)}) copy-start(f32[6,256,512]{2,1,0:T(8,128)} %param.4) | copy-start | bytes 9437188
